TPU v7x, 256 devices: a whole 4x4x8 slice. The times are simulated.
256 devices in a mesh: seq: 32 (over z_lo, x, y), head: 8 (over z_hi, core).
Axes of the slice: x: 4, y: 4, z: 8 (z_hi: 4, z_lo: 2; z = z_hi * 2 + z_lo), core: 2. Of those that a mesh axis runs over, the one named last changes fastest.
Arguments:
- query_tokens: bfloat16 [40960, 3072], P(('seq', 'head')), may hold values from -6 to 6
- key_tokens: bfloat16 [40960, 3072], P(('seq', 'head')), may hold values from -6 to 6
- value_tokens: bfloat16 [40960, 3072], P(('seq', 'head')), may hold values from -6 to 6
- matching: int32 [2, 32], replicated, may hold values from 0 to 31, as said below
Outputs:
- attended: bfloat16 [40960, 3072], P(('seq', 'head'))
Inputs may be any that keep to these rules, and one draw needn't show every extreme that they name: For each round r and block b: matching[r, matching[r, b]] == b and matching[r, b] != b; the 2 rows give every block different partners.
All inputs are finite; a program needn't handle non-finite values.
Results may differ from a plain program's by a relative error of at most 0.0048.
Values may be sent and summed in bfloat16 or wider, within the bound.
A program may use at most 64 MiB of HBM per device.

v0:
```python
import math
import jax
import jax.numpy as jnp
from jax import lax
from jax.sharding import PartitionSpec as P

HEAD_DIM = 128
ROUNDS = 2


def attend(query_rows, key_rows, value_rows, head_size):
    row_count, feature_width = query_rows.shape
    heads_here = feature_width // head_size
    block_rows = math.gcd(row_count, 512)
    score_scale = 1.0 / math.sqrt(head_size)
    key_heads = key_rows.reshape(-1, heads_here, head_size)
    value_heads = value_rows.reshape(-1, heads_here, head_size)
    query_blocks = query_rows.reshape(row_count // block_rows, block_rows, heads_here, head_size)

    def one_block(query_block):
        scores = (
            jnp.einsum("qhd,khd->hqk", query_block, key_heads, preferred_element_type=jnp.float32)
            * score_scale
        )
        weights = jnp.exp(scores - jnp.max(scores, axis=-1, keepdims=True))
        totals = jnp.sum(weights, axis=-1)
        mixed = jnp.einsum(
            "hqk,khd->qhd",
            weights.astype(jnp.bfloat16),
            value_heads,
            preferred_element_type=jnp.float32,
        )
        return (mixed / jnp.transpose(totals)[:, :, None]).astype(jnp.bfloat16)

    return lax.map(one_block, query_blocks).reshape(row_count, feature_width)


def per_device(query_tokens, key_tokens, value_tokens, matching):
    seq_count = lax.axis_size("seq")
    local_query, local_keys, local_values = (
        lax.all_to_all(query_tokens, "head", split_axis=1, concat_axis=0, tiled=True),
        lax.all_to_all(key_tokens, "head", split_axis=1, concat_axis=0, tiled=True),
        lax.all_to_all(value_tokens, "head", split_axis=1, concat_axis=0, tiled=True),
    )
    block_count, feature_width = local_keys.shape
    piece_rows = block_count // seq_count
    spread_keys, spread_values = (
        lax.all_to_all(
            local_keys.reshape(seq_count, piece_rows, feature_width),
            "seq",
            split_axis=0,
            concat_axis=0,
            tiled=True,
        ),
        lax.all_to_all(
            local_values.reshape(seq_count, piece_rows, feature_width),
            "seq",
            split_axis=0,
            concat_axis=0,
            tiled=True,
        ),
    )
    key_parts = []
    value_parts = []
    for round_index in range(ROUNDS):
        got_keys, got_values = (
            lax.all_to_all(
                jnp.take(spread_keys, matching[round_index], axis=0),
                "seq",
                split_axis=0,
                concat_axis=0,
                tiled=True,
            ),
            lax.all_to_all(
                jnp.take(spread_values, matching[round_index], axis=0),
                "seq",
                split_axis=0,
                concat_axis=0,
                tiled=True,
            ),
        )
        key_parts.append(got_keys.reshape(block_count, feature_width))
        value_parts.append(got_values.reshape(block_count, feature_width))
    partner_keys = jnp.concatenate(key_parts, 0)
    partner_values = jnp.concatenate(value_parts, 0)
    key_rows = jnp.concatenate([local_keys, partner_keys], 0)
    value_rows = jnp.concatenate([local_values, partner_values], 0)
    attended = attend(local_query, key_rows, value_rows, HEAD_DIM)
    return lax.all_to_all(attended, "head", split_axis=0, concat_axis=1, tiled=True)


def solution(mesh):
    return jax.shard_map(
        per_device,
        mesh=mesh,
        in_specs=(
            P(("seq", "head"), None),
            P(("seq", "head"), None),
            P(("seq", "head"), None),
            P(),
        ),
        out_specs=P(("seq", "head"), None),
        check_vma=False,
    )
```

profile of v0, /device:TPU:2, one launch (start us, length us, event | category | flops | bytes accessed | tf_op | source)
XLA Modules:
  0.0 343.2 jit_solution(16645471671025664687)
XLA Ops:
  0.0 0.0 copy-start.2
  0.0 2.3 copy.36
  2.3 8.5 %all-to-all-start.1 = ((bf16[160,8,384]{2,0,1:T(8,128)(2,1)}), bf16[160,8,384]{2,0,1:T(8,128)(2,1)S(1)}, u32[]{:S(2)}, u32[]{:S(2)}) async-start(bf16[160,8,384]{2,0,1:T(8,128)(2,1)} %bitcast.48), calls=%async_computation.1 | async-start | bytes 1966080 | tf_op jit(solution)/shard_map/all_to_all | solution.py:42
  10.8 0.0 copy-done.2
  10.8 0.1 copy.35
  10.9 27.8 %all-to-all-done.1 = bf16[160,8,384]{2,0,1:T(8,128)(2,1)S(1)} async-done(((bf16[160,8,384]{2,0,1:T(8,128)(2,1)}), bf16[160,8,384]{2,0,1:T(8,128)(2,1)S(1)}, u32[]{:S(2)}, u32[]{:S(2)}) %all-to-all-start.1) | async-done | bytes 983072 | tf_op jit(solution)/shard_map/all_to_all | solution.py:42
  38.7 31.0 %all_to_all.97 = bf16[160,8,384]{2,0,1:T(8,128)(2,1)} all-to-all(bf16[160,8,384]{2,0,1:T(8,128)(2,1)S(1)} %bitcast.65), channel_id=1, replica_groups=mesh['seq'=32,'head'=8] {'head'}, dimensions={1} | all-to-all | bytes 1966080 | tf_op jit(solution)/shard_map/all_to_all | solution.py:43
  69.7 21.4 %all_to_all.98 = bf16[32,40,384]{2,1,0:T(8,128)(2,1)S(1)} all-to-all(bf16[32,40,384]{2,1,0:T(8,128)(2,1)S(1)} %bitcast.62), channel_id=1, replica_groups=mesh['seq'=32,'head'=8] {'seq'}, dimensions={0} | all-to-all | bytes 1966080 | tf_op jit(solution)/shard_map/all_to_all | solution.py:48
  91.1 5.6 %all-to-all-start.6 = ((bf16[32,40,384]{2,1,0:T(8,128)(2,1)}), bf16[32,40,384]{2,1,0:T(8,128)(2,1)S(1)}, u32[]{:S(2)}, u32[]{:S(2)}) async-start(bf16[32,40,384]{2,1,0:T(8,128)(2,1)} %bitcast.10), calls=%async_computation.6 | async-start | bytes 1966080 | tf_op jit(solution)/shard_map/all_to_all | solution.py:55
  96.7 2.2 copy.37
  99.0 10.1 %all-to-all-done.6 = bf16[32,40,384]{2,1,0:T(8,128)(2,1)S(1)} async-done(((bf16[32,40,384]{2,1,0:T(8,128)(2,1)}), bf16[32,40,384]{2,1,0:T(8,128)(2,1)S(1)}, u32[]{:S(2)}, u32[]{:S(2)}) %all-to-all-start.6) | async-done | bytes 983072 | tf_op jit(solution)/shard_map/all_to_all | solution.py:55
  109.1 4.6 %all-to-all-start = ((bf16[160,8,384]{2,0,1:T(8,128)(2,1)}), bf16[160,8,384]{2,0,1:T(8,128)(2,1)}, u32[]{:S(2)}, u32[]{:S(2)}) async-start(bf16[160,8,384]{2,0,1:T(8,128)(2,1)} %bitcast.64), calls=%async_computation | async-start | bytes 1966080 | tf_op jit(solution)/shard_map/all_to_all | solution.py:41
  113.7 0.0 copy-done.3
  113.7 1.6 gather_fusion
  115.4 1.7 gather_fusion.2
  117.0 3.1 broadcast_select_fusion.2
  120.1 21.9 %all-to-all-done = bf16[160,8,384]{2,0,1:T(8,128)(2,1)} async-done(((bf16[160,8,384]{2,0,1:T(8,128)(2,1)}), bf16[160,8,384]{2,0,1:T(8,128)(2,1)}, u32[]{:S(2)}, u32[]{:S(2)}) %all-to-all-start) | async-done | bytes 983072 | tf_op jit(solution)/shard_map/all_to_all | solution.py:41
  142.0 5.3 %all-to-all-start.3 = ((bf16[32,40,384]{2,1,0:T(8,128)(2,1)}), bf16[32,40,384]{2,1,0:T(8,128)(2,1)}, u32[]{:S(2)}, u32[]{:S(2)}) async-start(bf16[32,40,384]{2,1,0:T(8,128)(2,1)} %get-tuple-element.68), calls=%async_computation.3 | async-start | bytes 1966080 | tf_op jit(solution)/shard_map/all_to_all | solution.py:67
  147.3 1.7 gather_fusion.1
  149.0 1.6 gather_fusion.3
  150.6 2.8 broadcast_select_fusion
  153.4 8.9 %all-to-all-done.3 = bf16[32,40,384]{2,1,0:T(8,128)(2,1)} async-done(((bf16[32,40,384]{2,1,0:T(8,128)(2,1)}), bf16[32,40,384]{2,1,0:T(8,128)(2,1)}, u32[]{:S(2)}, u32[]{:S(2)}) %all-to-all-start.3) | async-done | bytes 983072 | tf_op jit(solution)/shard_map/all_to_all | solution.py:67
  162.3 19.4 %all_to_all.99 = bf16[32,40,384]{2,1,0:T(8,128)(2,1)} all-to-all(bf16[32,40,384]{2,1,0:T(8,128)(2,1)S(1)} %get-tuple-element.70), channel_id=1, replica_groups=mesh['seq'=32,'head'=8] {'seq'}, dimensions={0} | all-to-all | bytes 1966080 | tf_op jit(solution)/shard_map/all_to_all | solution.py:67
  181.7 0.0 copy-done
  181.7 18.4 %all_to_all.100 = bf16[32,40,384]{2,1,0:T(8,128)(2,1)} all-to-all(bf16[32,40,384]{2,1,0:T(8,128)(2,1)S(1)} %copy-done), channel_id=1, replica_groups=mesh['seq'=32,'head'=8] {'seq'}, dimensions={0} | all-to-all | bytes 1966080 | tf_op jit(solution)/shard_map/all_to_all | solution.py:74
  200.1 5.8 %all-to-all-start.8 = ((bf16[32,40,384]{2,1,0:T(8,128)(2,1)}), bf16[32,40,384]{2,1,0:T(8,128)(2,1)}, u32[]{:S(2)}, u32[]{:S(2)}) async-start(bf16[32,40,384]{2,1,0:T(8,128)(2,1)} %get-tuple-element.69), calls=%async_computation.8 | async-start | bytes 1966080 | tf_op jit(solution)/shard_map/all_to_all | solution.py:74
  206.0 0.3 concatenate.20
  206.3 3.7 %concatenate.24 = bf16[1280,3,128]{2,1,0:T(4,128)(2,1)} reshape(bf16[8,160,384]{2,1,0:T(8,128)(2,1)} %bitcast.9) | data formatting | bytes 1966080 | tf_op jit(solution)/shard_map/concatenate | solution.py:87
  210.0 2.6 reshape.51
  212.7 1.2 copy.23
  213.8 2.6 concatenate.21
  216.5 3.7 %concatenate.22 = bf16[1280,3,128]{2,1,0:T(4,128)(2,1)} reshape(bf16[32,40,384]{2,1,0:T(8,128)(2,1)} %all_to_all.99) | data formatting | bytes 1966080 | tf_op jit(solution)/shard_map/concatenate | solution.py:86
  220.2 26.4 %pad_maximum_fusion = bf16[3840,3,128]{2,1,0:T(4,128)(2,1)S(1)} fusion(bf16[1280,3,128]{2,1,0:T(4,128)(2,1)} %concatenate.22, bf16[1280,3,128]{2,1,0:T(4,128)(2,1)S(1)} %concatenate.21, bf16[1280,3,128]{2,1,0:T(4,128)(2,1)S(1)} %concatenate.20), kind=kLoop, calls=%fused_computation.21 | loop fusion | flops 2949120 | bytes 5898240 | tf_op jit(solution)/shard_map/concatenate | solution.py:86
  246.6 0.4 copy.24
  247.1 3.7 %concatenate.25 = bf16[1280,3,128]{2,1,0:T(4,128)(2,1)} reshape(bf16[32,40,384]{2,1,0:T(8,128)(2,1)} %all_to_all.100) | data formatting | bytes 1966080 | tf_op jit(solution)/shard_map/concatenate | solution.py:87
  250.7 0.0 all-to-all-done.8
  250.7 3.7 %concatenate.26 = bf16[1280,3,128]{2,1,0:T(4,128)(2,1)} reshape(bf16[32,40,384]{2,1,0:T(8,128)(2,1)} %all-to-all-done.8) | data formatting | bytes 1966080 | tf_op jit(solution)/shard_map/concatenate | solution.py:87
  254.4 11.2 %pad_maximum_fusion.1 = bf16[3840,3,128]{2,1,0:T(4,128)(2,1)S(1)} fusion(bf16[1280,3,128]{2,1,0:T(4,128)(2,1)} %concatenate.26, bf16[1280,3,128]{2,1,0:T(4,128)(2,1)} %concatenate.25, bf16[1280,3,128]{2,1,0:T(4,128)(2,1)} %concatenate.24), kind=kLoop, calls=%fused_computation.22 | loop fusion | flops 2949120 | bytes 5898240 | tf_op jit(solution)/shard_map/concatenate | solution.py:87
  265.6 2.0 copy.25
  267.6 40.9 %while.10 = (s32[]{:T(128)}, bf16[5,256,3,128]{3,1,2,0:T(8,128)(2,1)}, bf16[5,256,3,128]{3,1,2,0:T(8,128)(2,1)}, bf16[3840,3,128]{2,0,1:T(8,128)(2,1)S(1)}, bf16[3840,3,128]{2,0,1:T(8,128)(2,1)}, /*index=5*/s32[]{:T(128)}) while((s32[]{:T(128)}, bf16[5,256,3,128]{3,1,2,0:T(8,128)(2,1)}, bf16[5,256,3,128]{3,1,2,0:T(8,128)(2,1)}, ...), condition=%wide.region_3.5_spmd, body=%wide.region_0.4_spmd.sunk | while | flops 1533737472 | bytes 53493856 | solution.py:35
  267.6 2.7 multiply_reduce_fusion.2
  270.3 2.1 fusion.36
  272.4 0.0 copy-done.1
  272.4 3.4 fusion.37
  275.8 2.7 multiply_reduce_fusion.2
  278.5 2.1 fusion.36
  280.6 0.0 copy-done.1
  280.6 3.4 fusion.37
  284.0 2.7 multiply_reduce_fusion.2
  286.7 2.1 fusion.36
  288.7 0.0 copy-done.1
  288.7 3.4 fusion.37
  292.2 2.7 multiply_reduce_fusion.2
  294.9 2.1 fusion.36
  296.9 0.0 copy-done.1
  296.9 3.4 fusion.37
  300.3 2.7 multiply_reduce_fusion.2
  303.1 2.1 fusion.36
  305.1 0.0 copy-done.1
  305.1 3.4 fusion.37
  308.5 2.0 copy.26
  310.6 0.9 all_to_all.83
  311.4 30.6 %all_to_all.101 = bf16[8,160,384]{2,1,0:T(8,128)(2,1)S(1)} all-to-all(bf16[8,160,384]{2,1,0:T(8,128)(2,1)S(1)} %all_to_all.83), channel_id=1, replica_groups=mesh['seq'=32,'head'=8] {'head'}, dimensions={0} | all-to-all | bytes 1966080 | tf_op jit(solution)/shard_map/all_to_all | solution.py:89
  342.1 1.1 copy.31
  (11 shorter events, 0.0 us)
Async XLA Ops:
  0.0 10.8 %copy-start.2 = (bf16[160,3072]{1,0:T(8,128)(2,1)S(1)}, bf16[160,3072]{1,0:T(8,128)(2,1)}, u32[]{:S(2)}) copy-start(bf16[160,3072]{1,0:T(8,128)(2,1)} %param.10) | copy-start | bytes 2949124
  2.3 36.4 %all-to-all-start.1 = ((bf16[160,8,384]{2,0,1:T(8,128)(2,1)}), bf16[160,8,384]{2,0,1:T(8,128)(2,1)S(1)}, u32[]{:S(2)}, u32[]{:S(2)}) async-start(bf16[160,8,384]{2,0,1:T(8,128)(2,1)} %bitcast.48), calls=%async_computation.1 | async-start | bytes 1966080 | tf_op jit(solution)/shard_map/all_to_all | solution.py:42
  69.7 44.0 %copy-start.3 = (s32[2,32]{1,0:T(2,128)S(1)}, s32[2,32]{1,0:T(2,128)}, u32[]{:S(2)}) copy-start(s32[2,32]{1,0:T(2,128)} %param.11) | copy-start | bytes 772
  91.1 18.0 %all-to-all-start.6 = ((bf16[32,40,384]{2,1,0:T(8,128)(2,1)}), bf16[32,40,384]{2,1,0:T(8,128)(2,1)S(1)}, u32[]{:S(2)}, u32[]{:S(2)}) async-start(bf16[32,40,384]{2,1,0:T(8,128)(2,1)} %bitcast.10), calls=%async_computation.6 | async-start | bytes 1966080 | tf_op jit(solution)/shard_map/all_to_all | solution.py:55
  109.1 32.9 %all-to-all-start = ((bf16[160,8,384]{2,0,1:T(8,128)(2,1)}), bf16[160,8,384]{2,0,1:T(8,128)(2,1)}, u32[]{:S(2)}, u32[]{:S(2)}) async-start(bf16[160,8,384]{2,0,1:T(8,128)(2,1)} %bitcast.64), calls=%async_computation | async-start | bytes 1966080 | tf_op jit(solution)/shard_map/all_to_all | solution.py:41
  142.0 20.3 %all-to-all-start.3 = ((bf16[32,40,384]{2,1,0:T(8,128)(2,1)}), bf16[32,40,384]{2,1,0:T(8,128)(2,1)}, u32[]{:S(2)}, u32[]{:S(2)}) async-start(bf16[32,40,384]{2,1,0:T(8,128)(2,1)} %get-tuple-element.68), calls=%async_computation.3 | async-start | bytes 1966080 | tf_op jit(solution)/shard_map/all_to_all | solution.py:67
  149.0 32.7 %copy-start = (bf16[32,40,384]{2,1,0:T(8,128)(2,1)S(1)}, bf16[32,40,384]{2,1,0:T(8,128)(2,1)}, u32[]{:S(2)}) copy-start(bf16[32,40,384]{2,1,0:T(8,128)(2,1)} %get-tuple-element.67) | copy-start | bytes 2949124
  200.1 50.6 %all-to-all-start.8 = ((bf16[32,40,384]{2,1,0:T(8,128)(2,1)}), bf16[32,40,384]{2,1,0:T(8,128)(2,1)}, u32[]{:S(2)}, u32[]{:S(2)}) async-start(bf16[32,40,384]{2,1,0:T(8,128)(2,1)} %get-tuple-element.69), calls=%async_computation.8 | async-start | bytes 1966080 | tf_op jit(solution)/shard_map/all_to_all | solution.py:74
  270.3 2.1 copy-start.1
  278.5 2.1 copy-start.1
  286.7 2.1 copy-start.1
  294.9 2.1 copy-start.1
  303.0 2.1 copy-start.1
where the time goes:
time: 345 us; the launch traced here: 343 us
  blocking collectives  121 us (35%)
  waiting for transfers between devices  68.7 us (20%)
  other arithmetic  53.7 us (16%)
  local copies, waits for them, and re-layouts  39.4 us (11%)
  matrix products  30.6 us (9%)
  starting transfers between devices  29.8 us (9%)
    all_to_all x1, blocking collectives, per_device(): lax.all_to_all(value_tokens, 'head', split_axis=1, concat_axis=0, tiled=T...  31 us
    all_to_all x1, blocking collectives, per_device(): lax.all_to_all(attended, 'head', split_axis=0, concat_axis=1, tiled=True)  30.6 us
    all_to_all x1, waiting for transfers between devices, per_device(): lax.all_to_all(key_tokens, 'head', split_axis=1, concat_axis=0, tiled=True)  27.8 us
    concatenate x1, other arithmetic, per_device(): key_rows = jnp.concatenate([local_keys, partner_keys], 0)  26.4 us
    all_to_all x1, waiting for transfers between devices, per_device(): lax.all_to_all(query_tokens, 'head', split_axis=1, concat_axis=0, tiled=T...  21.9 us
    all_to_all x1, blocking collectives, per_device(): lax.all_to_all(local_keys.reshape(seq_count, piece_rows, feature_width),...  21.4 us
    all_to_all x1, blocking collectives, per_device(): lax.all_to_all(jnp.take(spread_keys, matching[round_index], axis=0), 'seq...  19.4 us
    all_to_all x1, blocking collectives, per_device(): lax.all_to_all(jnp.take(spread_values, matching[round_index], axis=0), 's...  18.4 us
  transfers between devices with their start and end apart: 5, of which 4 were waited for; matrix products, arithmetic and copies ran while one was open for 17% of the time, Pallas kernels for 0%

commit v1 on v0

--- a/solution.py
+++ b/solution.py
@@ -6,6 +6,13 @@
 
 HEAD_DIM = 128
 ROUNDS = 2
+
+
+def exchange_blocks(array, name, split, join):
+    size = lax.axis_size(name)
+    blocks = jnp.stack(jnp.split(array, size, axis=split), axis=0)
+    blocks = lax.all_to_all(blocks, name, split_axis=0, concat_axis=0)
+    return jnp.concatenate(blocks, axis=join)
 
 
 def attend(query_rows, key_rows, value_rows, head_size):
@@ -40,7 +47,7 @@
     local_query, local_keys, local_values = (
         lax.all_to_all(query_tokens, "head", split_axis=1, concat_axis=0, tiled=True),
         lax.all_to_all(key_tokens, "head", split_axis=1, concat_axis=0, tiled=True),
-        lax.all_to_all(value_tokens, "head", split_axis=1, concat_axis=0, tiled=True),
+        exchange_blocks(value_tokens, "head", 1, 0),
     )
     block_count, feature_width = local_keys.shape
     piece_rows = block_count // seq_count

time: 345 us -> 358 us (1.038)
  local copies, waits for them, and re-layouts: 39.4 us -> 47.2 us
  other arithmetic: 53.7 us -> 59.2 us
    unnamed x6 -> x15, local copies, waits for them, and re-layouts: 0.01 us -> 11 us
    all_to_all x1, waiting for transfers between devices: 8.88 us -> 0.01 us  [per_device(): lax.all_to_all(jnp.take(spread_keys, matching[round_index], axis=0), 'seq...]
    all_to_all x1, waiting for transfers between devices: 0.01 us -> 8.47 us  [per_device(): lax.all_to_all(jnp.take(spread_values, matching[round_index], axis=0), 's...]
    concatenate x3, local copies, waits for them, and re-layouts: 11.1 us -> 5.19 us  [per_device(): value_rows = jnp.concatenate([local_values, partner_values], 0)]
    concatenate x1, other arithmetic: 11.2 us -> 16.3 us  [per_device(): value_rows = jnp.concatenate([local_values, partner_values], 0)]
  transfers between devices with their start and end apart: 5 -> 5, of which waited for: 4 -> 4; matrix products, arithmetic and copies ran while one was open for 17% -> 14% of each run, Pallas kernels for 0% -> 0%
where the time goes in v1:
time: 358 us; the launch traced here: 357 us
  blocking collectives  121 us (34%)
  waiting for transfers between devices  68.3 us (19%)
  other arithmetic  59.2 us (17%)
  local copies, waits for them, and re-layouts  47.2 us (13%)
  matrix products  30.6 us (9%)
  starting transfers between devices  29.8 us (8%)
    all_to_all x1, blocking collectives, per_device(): lax.all_to_all(key_tokens, 'head', split_axis=1, concat_axis=0, tiled=True)  31 us
    all_to_all x1, blocking collectives, per_device(): lax.all_to_all(attended, 'head', split_axis=0, concat_axis=1, tiled=True)  30.6 us
    all_to_all x1, waiting for transfers between devices, exchange_blocks(): blocks = lax.all_to_all(blocks, name, split_axis=0, concat_axis=0)  27.8 us
    concatenate x1, other arithmetic, per_device(): key_rows = jnp.concatenate([local_keys, partner_keys], 0)  26.4 us
    all_to_all x1, waiting for transfers between devices, per_device(): lax.all_to_all(query_tokens, 'head', split_axis=1, concat_axis=0, tiled=T...  21.9 us
    all_to_all x1, blocking collectives, per_device(): lax.all_to_all(local_values.reshape(seq_count, piece_rows, feature_width)...  21.4 us
    all_to_all x1, blocking collectives, per_device(): lax.all_to_all(jnp.take(spread_values, matching[round_index], axis=0), 's...  19.5 us
    all_to_all x1, blocking collectives, per_device(): lax.all_to_all(jnp.take(spread_keys, matching[round_index], axis=0), 'seq...  18.4 us
  transfers between devices with their start and end apart: 5, of which 4 were waited for; matrix products, arithmetic and copies ran while one was open for 14% of the time, Pallas kernels for 0%

profile of v1, /device:TPU:2, one launch (start us, length us, event | category | flops | bytes accessed | tf_op | source)
XLA Modules:
  0.0 356.6 jit_solution(10639120948624782407)
XLA Ops:
  0.0 1.6 bitcast_dynamic-update-slice_fusion.7
  1.6 1.6 bitcast_dynamic-update-slice_fusion.6
  3.2 1.6 bitcast_dynamic-update-slice_fusion.5
  4.8 1.6 bitcast_dynamic-update-slice_fusion.4
  6.3 1.6 bitcast_dynamic-update-slice_fusion.3
  7.9 1.6 bitcast_dynamic-update-slice_fusion.2
  9.5 1.6 bitcast_dynamic-update-slice_fusion.1
  11.0 1.6 bitcast_dynamic-update-slice_fusion
  12.6 8.5 %all-to-all-start.5 = ((bf16[8,160,384]{2,1,0:T(8,128)(2,1)}), bf16[8,160,384]{2,1,0:T(8,128)(2,1)S(1)}, u32[]{:S(2)}, u32[]{:S(2)}) async-start(bf16[8,160,384]{2,1,0:T(8,128)(2,1)} %bitcast_dynamic-update-slice_fusion), calls=%async_computation.5 | async-start | bytes 1966080 | tf_op jit(solution)/shard_map/all_to_all | solution.py:14
  21.1 0.1 copy.30
  21.2 27.8 %all-to-all-done.5 = bf16[8,160,384]{2,1,0:T(8,128)(2,1)S(1)} async-done(((bf16[8,160,384]{2,1,0:T(8,128)(2,1)}), bf16[8,160,384]{2,1,0:T(8,128)(2,1)S(1)}, u32[]{:S(2)}, u32[]{:S(2)}) %all-to-all-start.5) | async-done | bytes 983072 | tf_op jit(solution)/shard_map/all_to_all | solution.py:14
  48.9 31.0 %all_to_all.86 = bf16[160,8,384]{2,0,1:T(8,128)(2,1)} all-to-all(bf16[160,8,384]{2,0,1:T(8,128)(2,1)S(1)} %bitcast.74), channel_id=1, replica_groups=mesh['seq'=32,'head'=8] {'head'}, dimensions={1} | all-to-all | bytes 1966080 | tf_op jit(solution)/shard_map/all_to_all | solution.py:49
  79.9 21.4 %all_to_all.87 = bf16[32,40,384]{2,1,0:T(8,128)(2,1)S(1)} all-to-all(bf16[32,40,384]{2,1,0:T(8,128)(2,1)S(1)} %bitcast.72), channel_id=1, replica_groups=mesh['seq'=32,'head'=8] {'seq'}, dimensions={0} | all-to-all | bytes 1966080 | tf_op jit(solution)/shard_map/all_to_all | solution.py:62
  101.3 5.6 %all-to-all-start.2 = ((bf16[32,40,384]{2,1,0:T(8,128)(2,1)}), bf16[32,40,384]{2,1,0:T(8,128)(2,1)S(1)}, u32[]{:S(2)}, u32[]{:S(2)}) async-start(bf16[32,40,384]{2,1,0:T(8,128)(2,1)} %bitcast.7), calls=%async_computation.2 | async-start | bytes 1966080 | tf_op jit(solution)/shard_map/all_to_all | solution.py:55
  107.0 2.2 copy.31
  109.2 10.1 %all-to-all-done.2 = bf16[32,40,384]{2,1,0:T(8,128)(2,1)S(1)} async-done(((bf16[32,40,384]{2,1,0:T(8,128)(2,1)}), bf16[32,40,384]{2,1,0:T(8,128)(2,1)S(1)}, u32[]{:S(2)}, u32[]{:S(2)}) %all-to-all-start.2) | async-done | bytes 983072 | tf_op jit(solution)/shard_map/all_to_all | solution.py:55
  119.3 4.6 %all-to-all-start = ((bf16[160,8,384]{2,0,1:T(8,128)(2,1)}), bf16[160,8,384]{2,0,1:T(8,128)(2,1)}, u32[]{:S(2)}, u32[]{:S(2)}) async-start(bf16[160,8,384]{2,0,1:T(8,128)(2,1)} %bitcast.73), calls=%async_computation | async-start | bytes 1966080 | tf_op jit(solution)/shard_map/all_to_all | solution.py:48
  124.0 1.6 gather_fusion.2
  125.6 1.6 gather_fusion
  127.3 3.1 broadcast_select_fusion.2
  130.4 21.9 %all-to-all-done = bf16[160,8,384]{2,0,1:T(8,128)(2,1)} async-done(((bf16[160,8,384]{2,0,1:T(8,128)(2,1)}), bf16[160,8,384]{2,0,1:T(8,128)(2,1)}, u32[]{:S(2)}, u32[]{:S(2)}) %all-to-all-start) | async-done | bytes 983072 | tf_op jit(solution)/shard_map/all_to_all | solution.py:48
  152.2 5.3 %all-to-all-start.7 = ((bf16[32,40,384]{2,1,0:T(8,128)(2,1)}), bf16[32,40,384]{2,1,0:T(8,128)(2,1)}, u32[]{:S(2)}, u32[]{:S(2)}) async-start(bf16[32,40,384]{2,1,0:T(8,128)(2,1)} %get-tuple-element.67), calls=%async_computation.7 | async-start | bytes 1966080 | tf_op jit(solution)/shard_map/all_to_all | solution.py:81
  157.6 1.6 gather_fusion.3
  159.2 1.7 gather_fusion.1
  160.9 3.1 broadcast_select_fusion
  164.1 8.5 %all-to-all-done.7 = bf16[32,40,384]{2,1,0:T(8,128)(2,1)} async-done(((bf16[32,40,384]{2,1,0:T(8,128)(2,1)}), bf16[32,40,384]{2,1,0:T(8,128)(2,1)}, u32[]{:S(2)}, u32[]{:S(2)}) %all-to-all-start.7) | async-done | bytes 983072 | tf_op jit(solution)/shard_map/all_to_all | solution.py:81
  172.5 19.5 %all_to_all.88 = bf16[32,40,384]{2,1,0:T(8,128)(2,1)S(1)} all-to-all(bf16[32,40,384]{2,1,0:T(8,128)(2,1)} %get-tuple-element.69), channel_id=1, replica_groups=mesh['seq'=32,'head'=8] {'seq'}, dimensions={0} | all-to-all | bytes 1966080 | tf_op jit(solution)/shard_map/all_to_all | solution.py:81
  192.1 18.4 %all_to_all.89 = bf16[32,40,384]{2,1,0:T(8,128)(2,1)} all-to-all(bf16[32,40,384]{2,1,0:T(8,128)(2,1)S(1)} %copy-done.1), channel_id=1, replica_groups=mesh['seq'=32,'head'=8] {'seq'}, dimensions={0} | all-to-all | bytes 1966080 | tf_op jit(solution)/shard_map/all_to_all | solution.py:74
  210.5 5.8 %all-to-all-start.4 = ((bf16[32,40,384]{2,1,0:T(8,128)(2,1)}), bf16[32,40,384]{2,1,0:T(8,128)(2,1)}, u32[]{:S(2)}, u32[]{:S(2)}) async-start(bf16[32,40,384]{2,1,0:T(8,128)(2,1)} %get-tuple-element.70), calls=%async_computation.4 | async-start | bytes 1966080 | tf_op jit(solution)/shard_map/all_to_all | solution.py:74
  216.3 3.7 %concatenate.20 = bf16[1280,3,128]{2,1,0:T(4,128)(2,1)} reshape(bf16[8,160,384]{2,1,0:T(8,128)(2,1)} %bitcast.5) | data formatting | bytes 1966080 | tf_op jit(solution)/shard_map/concatenate | solution.py:93
  220.0 2.6 reshape.45
  222.7 1.2 copy.20
  223.9 0.3 concatenate.24
  224.2 3.7 %concatenate.25 = bf16[1280,3,128]{2,1,0:T(4,128)(2,1)} reshape(bf16[32,40,384]{2,1,0:T(8,128)(2,1)} %all-to-all-done.7) | data formatting | bytes 1966080 | tf_op jit(solution)/shard_map/concatenate | solution.py:94
  227.9 1.2 concatenate.26
  229.0 16.3 %pad_maximum_fusion.1 = bf16[3840,3,128]{2,1,0:T(4,128)(2,1)S(1)} fusion(bf16[1280,3,128]{2,1,0:T(4,128)(2,1)} %concatenate.26, bf16[1280,3,128]{2,1,0:T(4,128)(2,1)} %concatenate.25, bf16[1280,3,128]{2,1,0:T(4,128)(2,1)S(1)} %concatenate.24), kind=kLoop, calls=%fused_computation.22 | loop fusion | flops 2949120 | bytes 5898240 | tf_op jit(solution)/shard_map/concatenate | solution.py:94
  245.4 2.0 copy.22
  247.4 2.7 concatenate.21
  250.2 0.0 all-to-all-done.4
  250.2 3.7 %concatenate.22 = bf16[1280,3,128]{2,1,0:T(4,128)(2,1)} reshape(bf16[32,40,384]{2,1,0:T(8,128)(2,1)} %all-to-all-done.4) | data formatting | bytes 1966080 | tf_op jit(solution)/shard_map/concatenate | solution.py:93
  253.9 26.4 %pad_maximum_fusion = bf16[3840,3,128]{2,1,0:T(4,128)(2,1)S(1)} fusion(bf16[1280,3,128]{2,1,0:T(4,128)(2,1)} %concatenate.22, bf16[1280,3,128]{2,1,0:T(4,128)(2,1)S(1)} %concatenate.21, bf16[1280,3,128]{2,1,0:T(4,128)(2,1)S(1)} %copy-done), kind=kLoop, calls=%fused_computation.21 | loop fusion | flops 2949120 | bytes 5898240 | tf_op jit(solution)/shard_map/concatenate | solution.py:93
  280.3 0.4 copy.21
  280.7 41.2 %while.10 = (s32[]{:T(128)}, bf16[5,256,3,128]{3,1,2,0:T(8,128)(2,1)}, bf16[5,256,3,128]{3,1,2,0:T(8,128)(2,1)}, bf16[3840,3,128]{2,0,1:T(8,128)(2,1)S(1)}, bf16[3840,3,128]{2,0,1:T(8,128)(2,1)}, /*index=5*/s32[]{:T(128)}) while((s32[]{:T(128)}, bf16[5,256,3,128]{3,1,2,0:T(8,128)(2,1)}, bf16[5,256,3,128]{3,1,2,0:T(8,128)(2,1)}, ...), condition=%wide.region_3.5_spmd, body=%wide.region_0.4_spmd.sunk | while | flops 1533737472 | bytes 53493856 | solution.py:42
  281.0 2.7 multiply_reduce_fusion.2
  283.7 2.1 fusion.36
  285.8 3.4 fusion.37
  289.2 2.7 multiply_reduce_fusion.2
  291.9 2.1 fusion.36
  294.0 3.4 fusion.37
  297.4 2.7 multiply_reduce_fusion.2
  300.1 2.1 fusion.36
  302.1 0.0 copy-done.2
  302.2 3.4 fusion.37
  305.6 2.7 multiply_reduce_fusion.2
  308.3 2.1 fusion.36
  310.3 0.0 copy-done.2
  310.3 3.4 fusion.37
  313.7 2.7 multiply_reduce_fusion.2
  316.5 2.1 fusion.36
  318.5 3.4 fusion.37
  321.9 2.0 copy.23
  324.0 0.9 all_to_all.72
  324.8 30.6 %all_to_all.90 = bf16[8,160,384]{2,1,0:T(8,128)(2,1)S(1)} all-to-all(bf16[8,160,384]{2,1,0:T(8,128)(2,1)S(1)} %all_to_all.72), channel_id=1, replica_groups=mesh['seq'=32,'head'=8] {'head'}, dimensions={0} | all-to-all | bytes 1966080 | tf_op jit(solution)/shard_map/all_to_all | solution.py:96
  355.5 1.1 copy.27
  (20 shorter events, 0.1 us)
Async XLA Ops:
  0.0 21.0 %copy-start.3 = (bf16[160,3072]{1,0:T(8,128)(2,1)S(1)}, bf16[160,3072]{1,0:T(8,128)(2,1)}, u32[]{:S(2)}) copy-start(bf16[160,3072]{1,0:T(8,128)(2,1)} %param.9) | copy-start | bytes 2949124
  12.6 36.4 %all-to-all-start.5 = ((bf16[8,160,384]{2,1,0:T(8,128)(2,1)}), bf16[8,160,384]{2,1,0:T(8,128)(2,1)S(1)}, u32[]{:S(2)}, u32[]{:S(2)}) async-start(bf16[8,160,384]{2,1,0:T(8,128)(2,1)} %bitcast_dynamic-update-slice_fusion), calls=%async_computation.5 | async-start | bytes 1966080 | tf_op jit(solution)/shard_map/all_to_all | solution.py:14
  79.9 44.0 %copy-start.4 = (s32[2,32]{1,0:T(2,128)S(1)}, s32[2,32]{1,0:T(2,128)}, u32[]{:S(2)}) copy-start(s32[2,32]{1,0:T(2,128)} %param.11) | copy-start | bytes 772
  101.3 18.0 %all-to-all-start.2 = ((bf16[32,40,384]{2,1,0:T(8,128)(2,1)}), bf16[32,40,384]{2,1,0:T(8,128)(2,1)S(1)}, u32[]{:S(2)}, u32[]{:S(2)}) async-start(bf16[32,40,384]{2,1,0:T(8,128)(2,1)} %bitcast.7), calls=%async_computation.2 | async-start | bytes 1966080 | tf_op jit(solution)/shard_map/all_to_all | solution.py:55
  119.3 32.9 %all-to-all-start = ((bf16[160,8,384]{2,0,1:T(8,128)(2,1)}), bf16[160,8,384]{2,0,1:T(8,128)(2,1)}, u32[]{:S(2)}, u32[]{:S(2)}) async-start(bf16[160,8,384]{2,0,1:T(8,128)(2,1)} %bitcast.73), calls=%async_computation | async-start | bytes 1966080 | tf_op jit(solution)/shard_map/all_to_all | solution.py:48
  152.2 20.3 %all-to-all-start.7 = ((bf16[32,40,384]{2,1,0:T(8,128)(2,1)}), bf16[32,40,384]{2,1,0:T(8,128)(2,1)}, u32[]{:S(2)}, u32[]{:S(2)}) async-start(bf16[32,40,384]{2,1,0:T(8,128)(2,1)} %get-tuple-element.67), calls=%async_computation.7 | async-start | bytes 1966080 | tf_op jit(solution)/shard_map/all_to_all | solution.py:81
  159.2 32.9 %copy-start.1 = (bf16[32,40,384]{2,1,0:T(8,128)(2,1)S(1)}, bf16[32,40,384]{2,1,0:T(8,128)(2,1)}, u32[]{:S(2)}) copy-start(bf16[32,40,384]{2,1,0:T(8,128)(2,1)} %get-tuple-element.68) | copy-start | bytes 2949124
  210.5 39.7 %all-to-all-start.4 = ((bf16[32,40,384]{2,1,0:T(8,128)(2,1)}), bf16[32,40,384]{2,1,0:T(8,128)(2,1)}, u32[]{:S(2)}, u32[]{:S(2)}) async-start(bf16[32,40,384]{2,1,0:T(8,128)(2,1)} %get-tuple-element.70), calls=%async_computation.4 | async-start | bytes 1966080 | tf_op jit(solution)/shard_map/all_to_all | solution.py:74
  247.4 6.5 %copy-start = (bf16[1280,3,128]{2,1,0:T(4,128)(2,1)S(1)}, bf16[1280,3,128]{2,1,0:T(4,128)(2,1)}, u32[]{:S(2)}) copy-start(bf16[1280,3,128]{2,1,0:T(4,128)(2,1)} %concatenate.20) | copy-start | bytes 2949124
  283.7 2.1 copy-start.2
  291.9 2.1 copy-start.2
  300.1 2.1 copy-start.2
  308.3 2.1 copy-start.2
  316.4 2.1 copy-start.2
